TPU v7x, 32 devices: a whole 2x2x4 slice. The times are simulated.
32 devices in a mesh: area: 4 (over z), dev: 8 (over y, x, core).
Axes of the slice: x: 2, y: 2, z: 4, core: 2. Of those that a mesh axis runs over, the one named last changes fastest.
Arguments:
- wave_fwd: float32 [3, 16384, 128], P(None, ('area', 'dev')), may hold values from -6 to 6
- wave_bwd: float32 [3, 16384, 128], P(None, ('area', 'dev')), may hold values from -6 to 6
- seg_reflect: float32 [3, 16384], P(None, ('area', 'dev')), may hold values from 0.04 to 0.4
- seg_count: int32 [32, 64], P(('area', 'dev')), may hold values from 1 to 24, 512 in all within a row
- modal_admit: float32 [3, 2048], P(None, ('area', 'dev')), may hold values from 0.02 to 0.2
- modal_transform: float32 [3, 3], replicated, may hold values from -3.5 to 3.5
- end_slot: int32 [2048, 2], P(('area', 'dev')), may hold values from 0 to 255, as said below
- recv_bus: int32 [32, 256], P(('area', 'dev')), may hold values from -1 to 63, as said below
- bus_impedance: float32 [3, 3, 2048], P(None, None, ('area', 'dev')), as said below
- link_bus: int32 [192, 2], P('area'), may hold values from 0 to 511, as said below
- link_resist: float32 [192], P('area'), may hold values from 0.5 to 5
- source_current: float32 [4, 2048, 3, 128], P(None, ('area', 'dev')), may hold values from -6 to 6
Outputs:
- bus_voltage: float32 [4, 2048, 3, 128], P(None, ('area', 'dev'))
- final_fwd: float32 [3, 16384, 128], P(None, ('area', 'dev'))
- final_bwd: float32 [3, 16384, 128], P(None, ('area', 'dev'))
Inputs may be any that keep to these rules, and one draw needn't show every extreme that they name: `end_slot`: entry [l, s] is the slot of end s (0 sending, 1 receiving) of line l within its device's 32 blocks of 8 slots, block q // 8 going to owner device q // 8. The slots of one device are distinct. Every device fills all 8 slots of the block for some owner, and one owner receives 8 ends from every device. `recv_bus`: row r, column s * 8 + c: the local bus of device r to which slot c of device s's block for r attaches, and -1 exactly where no end of device s holds that slot. `link_bus`: the two buses of a link differ. `bus_impedance`: each bus's 3x3 matrix is symmetric with a positive diagonal larger than the sum of its row's other magnitudes.
All inputs are finite; a program needn't handle non-finite values.
Results may differ from a plain program's by a relative error of at most 0.00012.
Values sent between devices are 32-bit elements; how exact they have to be, the bound alone decides.
A program may use at most 64 MiB of HBM per device.

v0:
```python
import functools

import jax
import jax.numpy as jnp
from jax import lax
from jax.experimental import pallas as pl
from jax.experimental.pallas import tpu as pltpu
from jax.sharding import PartitionSpec as P

STEPS = 4
MESH = pl.DeviceIdType.MESH
F32 = jnp.float32
BF16 = jnp.bfloat16
EXACT = lax.Precision.HIGHEST


def iota(shape, dim):
    return lax.broadcasted_iota(jnp.int32, shape, dim)


def to_column(row):
    n = row.shape[1]
    eye = iota((n, n), 0) == iota((n, n), 1)
    return jnp.sum(jnp.where(eye, row, 0.0), axis=1, keepdims=True)


def to_row(column):
    n = column.shape[0]
    eye = iota((n, n), 0) == iota((n, n), 1)
    return jnp.sum(jnp.where(eye, column, 0.0), axis=0, keepdims=True)


def onehot(flag):
    return jnp.where(flag, 1.0, 0.0).astype(BF16)


def pick(matrix, value):
    n = value.shape[1]
    high = value.astype(BF16)
    low = (value - high.astype(F32)).astype(BF16)
    both = jnp.dot(
        matrix, jnp.concatenate([high, low], axis=1), preferred_element_type=F32
    )
    return both[:, :n] + both[:, n:]


def kernel(
    areas,
    devs,
    fwd_in,
    bwd_in,
    refl_ref,
    count_ref,
    admit_ref,
    trans_ref,
    slot_ref,
    recv_ref,
    imp_ref,
    link_ref,
    resist_ref,
    src_ref,
    volt_ref,
    fwd,
    bwd,
    h_send,
    h_recv,
    e_send,
    e_recv,
    g_recv,
    v_send,
    v_recv,
    imp_all,
    gb,
    gf,
    gbt,
    gft,
    rsum,
    rback,
    ct,
    cm,
    adm,
    zcol,
    keep_f,
    take_f,
    keep_b,
    take_b,
    arr,
    inj,
    minv,
    send_sem,
    recv_sem,
    imp_sem,
):
    total = areas * devs
    area, dev = lax.axis_index("area"), lax.axis_index("dev")
    me = area * devs + dev
    cases = fwd.shape[2]
    segs = fwd.shape[1]
    lines = slot_ref.shape[1]
    slots = recv_ref.shape[1]
    buses = imp_ref.shape[2]
    links = link_ref.shape[1]
    owners = links // 8
    cap = slots // total

    barrier = pltpu.get_barrier_semaphore()

    def peer_of(p):
        peer = lax.rem(me + p, total)
        return peer, (peer // devs, lax.rem(peer, devs))

    @pl.loop(1, total)
    def _(p):
        _, where = peer_of(p)
        pl.semaphore_signal(barrier, inc=1, device_id=where, device_id_type=MESH)

    def push_all(send, recv, phase, step):
        @pl.loop(1, total, unroll=total <= 32)
        def _(p):
            peer, where = peer_of(p)
            pltpu.make_async_remote_copy(
                src_ref=send.at[step, peer],
                dst_ref=recv.at[step, me],
                send_sem=send_sem.at[phase, step],
                recv_sem=recv_sem.at[phase, step],
                device_id=where,
                device_id_type=MESH,
            ).start()

    def push_shares(step):
        @pl.loop(0, owners)
        def _(other):
            @pl.when(other != dev)
            def _():
                pltpu.make_async_remote_copy(
                    src_ref=e_send.at[step, other],
                    dst_ref=e_recv.at[step, dev],
                    send_sem=send_sem.at[1, step],
                    recv_sem=recv_sem.at[1, step],
                    device_id=(area, other),
                    device_id_type=MESH,
                ).start()

    def sum_shares(step):
        e_recv[step, dev] = e_send[step, dev]
        wait(e_recv.at[step], devs - 1, recv_sem.at[1, step])
        g_recv[step, dev] = jnp.sum(e_recv[step], axis=0)

        @pl.loop(1, devs)
        def _(p):
            other = lax.rem(dev + p, devs)
            pltpu.make_async_remote_copy(
                src_ref=g_recv.at[step, dev],
                dst_ref=g_recv.at[step, dev],
                send_sem=send_sem.at[2, step],
                recv_sem=recv_sem.at[2, step],
                device_id=(area, other),
                device_id_type=MESH,
            ).start()

    def wait(buf, count, sem):
        ref = buf.at[pl.ds(0, count)]
        pltpu.make_async_copy(ref, ref, sem).wait()

    counts_row = count_ref[...].astype(F32)
    counts_col = to_column(counts_row)
    square = (lines, lines)
    first_col = jnp.sum(
        jnp.where(iota(square, 1) < iota(square, 0), counts_row, 0.0), axis=1, keepdims=True
    )
    first_row = to_row(first_col)
    last_col = first_col + counts_col - 1.0
    last_row = first_row + counts_row - 1.0
    slot0_row = slot_ref[0:1, :].astype(F32)
    slot1_row = slot_ref[1:2, :].astype(F32)
    slot0_col, slot1_col = to_column(slot0_row), to_column(slot1_row)
    seg_lane = iota((lines, segs), 1).astype(F32)
    seg_sub = iota((segs, lines), 0).astype(F32)
    slot_lane = iota((lines, slots), 1).astype(F32)
    slot_sub = iota((slots, lines), 0).astype(F32)
    q0, q1 = onehot(slot_sub == slot0_row), onehot(slot_sub == slot1_row)
    gb[...] = jnp.dot(q0, onehot(seg_lane == first_col), preferred_element_type=F32).astype(BF16)
    gf[...] = jnp.dot(q1, onehot(seg_lane == last_col), preferred_element_type=F32).astype(BF16)
    held = q0.astype(F32) + q1.astype(F32)
    for m in range(3):
        column = 2.0 * jnp.sum(held * admit_ref[m : m + 1, :], axis=1, keepdims=True)
        adm[m] = jnp.broadcast_to(column, (slots, cases))

    def gather_send(step):
        for m in range(3):
            arr[m] = pick(gb[...], bwd[m]) + pick(gf[...], fwd[m])
        for i in range(3):
            value = trans_ref[0, i] * (adm[0] * arr[0])
            value = value + trans_ref[1, i] * (adm[1] * arr[1])
            value = value + trans_ref[2, i] * (adm[2] * arr[2])
            h_send[step, :, :, i * cases : (i + 1) * cases] = value.reshape(total, cap, cases)
        push_all(h_send, h_recv, 0, step)
        h_recv[step, me] = h_send[step, me]

    fwd[...] = fwd_in[...]
    bwd[...] = bwd_in[...]
    pl.semaphore_wait(barrier, total - 1)

    @pl.loop(1, devs)
    def _(p):
        other = lax.rem(dev + p, devs)
        pltpu.make_async_remote_copy(
            src_ref=imp_ref,
            dst_ref=imp_all.at[dev],
            send_sem=imp_sem.at[0],
            recv_sem=imp_sem.at[1],
            device_id=(area, other),
            device_id_type=MESH,
        ).start()

    gather_send(0)
    imp_all[dev] = imp_ref[...]

    recv_row = recv_ref[...].astype(F32)
    rsum[...] = onehot(iota((buses, slots), 0).astype(F32) == recv_row)
    rback[...] = onehot(iota((slots, buses), 1).astype(F32) == to_column(recv_row))
    link0_row, link1_row = link_ref[0:1, :].astype(F32), link_ref[1:2, :].astype(F32)
    link0, link1 = to_column(link0_row), to_column(link1_row)

    def incidence(d):
        index = (iota((links, buses), 1) + d * buses).astype(F32)
        return jnp.where(index == link0, 1.0, 0.0) - jnp.where(index == link1, 1.0, 0.0)

    ct[...] = incidence(dev).astype(BF16)
    index = (iota((buses, links), 0) + dev * buses).astype(F32)
    cm[...] = (
        jnp.where(index == link0_row, 1.0, 0.0) - jnp.where(index == link1_row, 1.0, 0.0)
    ).astype(BF16)
    for ij in range(9):
        zcol[ij] = jnp.broadcast_to(to_column(imp_ref[ij // 3, ij % 3 : ij % 3 + 1, :]), (buses, cases))

    def wave_tables():
        fst = onehot(seg_sub == first_row)
        lst = onehot(seg_sub == last_row)
        gbt[...] = jnp.dot(fst, onehot(slot_lane == slot0_col), preferred_element_type=F32).astype(BF16)
        gft[...] = jnp.dot(lst, onehot(slot_lane == slot1_col), preferred_element_type=F32).astype(BF16)
        not_first = 1.0 - jnp.sum(fst.astype(F32), axis=1, keepdims=True)
        not_last = 1.0 - jnp.sum(lst.astype(F32), axis=1, keepdims=True)
        for m in range(3):
            r = to_column(refl_ref[m : m + 1, :])
            r_next = pltpu.roll(jnp.broadcast_to(r, (segs, cases)), segs - 1, 0)
            keep_f[m] = jnp.broadcast_to((1.0 - r) * not_first, (segs, cases))
            take_f[m] = jnp.broadcast_to(r * not_first, (segs, cases))
            keep_b[m] = (1.0 - r_next) * not_last
            take_b[m] = r_next * not_last

    def advance():
        for m in range(3):
            f, b = fwd[m], bwd[m]
            fwd[m] = keep_f[m] * pltpu.roll(f, 1, 0) + take_f[m] * b
            bwd[m] = keep_b[m] * pltpu.roll(b, segs - 1, 0) + take_b[m] * f

    wait(imp_all, devs - 1, imp_sem.at[1])
    minv[...] = jnp.zeros_like(minv)
    eye = iota((links, links), 0) == iota((links, links), 1)

    @pl.loop(0, devs)
    def _(d):
        c = incidence(d)
        for i in range(3):
            for j in range(i + 1):
                z = imp_all[d, i, j : j + 1, :]
                minv[i * links : (i + 1) * links, j * links : (j + 1) * links] += lax.dot_general(
                    c * z, c, (((1,), (1,)), ((), ())), precision=EXACT, preferred_element_type=F32
                )

    for i in range(3):
        span = slice(i * links, (i + 1) * links)
        minv[span, span] += jnp.where(eye, resist_ref[...], 0.0)
        for j in range(i):
            past = slice(j * links, (j + 1) * links)
            minv[past, span] = minv[span, past]
    order = 3 * links
    lane = iota((order, order), 1)

    @pl.loop(0, links)
    def _(n):
        spots = [n + u * links for u in range(3)]
        a = minv[...]
        rows = [minv[pl.ds(k, 1), :] for k in spots]
        here = [lane == k for k in spots]
        edge = [lane[:1] == k for k in spots]
        cols = [jnp.sum(jnp.where(h, a, 0.0), axis=1, keepdims=True) for h in here]
        block = [
            [jnp.sum(jnp.where(g, r, 0.0), axis=1, keepdims=True) for g in edge] for r in rows
        ]
        for v in range(3):
            inverse = 1.0 / block[v][v]
            row, col = rows[v], cols[v] * inverse
            a = a - col * row
            scaled = row * inverse
            factor = [block[u][v] for u in range(3)]
            across = [block[v][w] * inverse for w in range(3)]
            for u in range(3):
                rows[u] = scaled if u == v else rows[u] - factor[u] * scaled
                cols[u] = col if u == v else cols[u] - block[v][u] * col
            for u in range(3):
                for w in range(3):
                    if u != v and w != v:
                        block[u][w] = block[u][w] - factor[u] * across[w]
            for u in range(3):
                if u != v:
                    block[u][v], block[v][u] = factor[u] * inverse, across[u]
            block[v][v] = -inverse
        for u in range(3):
            a = jnp.where(here[u], cols[u], a)
            for w in range(3):
                rows[u] = jnp.where(edge[w], block[u][w], rows[u])
        minv[...] = a
        for u in range(3):
            minv[pl.ds(spots[u], 1), :] = rows[u]

    def apply(step, values):
        return [
            zcol[3 * i] * values[0] + zcol[3 * i + 1] * values[1] + zcol[3 * i + 2] * values[2]
            for i in range(3)
        ]

    def finish(step, begin=False):
        wait(h_recv.at[step], total - 1, recv_sem.at[0, step])
        for i in range(3):
            part = h_recv[step, :, :, i * cases : (i + 1) * cases].reshape(slots, cases)
            inj[i] = src_ref[step, i] + pick(rsum[...], part)
        open_volts = apply(step, [inj[i] for i in range(3)])
        for i in range(3):
            e_send[step, :, :, i * cases : (i + 1) * cases] = pick(
                ct[...], open_volts[i]
            ).reshape(owners, 8, cases)
        push_shares(step)

        @pl.when(dev < owners)
        def _():
            sum_shares(step)
            wait(g_recv.at[step], owners - 1, recv_sem.at[2, step])

        @pl.when(dev >= owners)
        def _():
            wait(g_recv.at[step], owners, recv_sem.at[2, step])

        stacked = jnp.concatenate(
            [
                g_recv[step, :, :, i * cases : (i + 1) * cases].reshape(links, cases)
                for i in range(3)
            ],
            axis=0,
        )
        current = jnp.dot(minv[...], stacked, precision=EXACT, preferred_element_type=F32)
        net = [
            inj[i] + pick(cm[...], current[i * links : (i + 1) * links]) for i in range(3)
        ]
        volts = apply(step, net)
        for i in range(3):
            volt_ref[step, i] = volts[i]
            v_send[step, :, :, i * cases : (i + 1) * cases] = pick(rback[...], volts[i]).reshape(
                total, cap, cases
            )
        push_all(v_send, v_recv, 3, step)
        v_recv[step, me] = v_send[step, me]
        if begin:
            wave_tables()
        advance()
        wait(v_recv.at[step], total - 1, recv_sem.at[3, step])
        ends = [
            v_recv[step, :, :, i * cases : (i + 1) * cases].reshape(slots, cases) for i in range(3)
        ]
        for m in range(3):
            out = trans_ref[m, 0] * ends[0] + trans_ref[m, 1] * ends[1] + trans_ref[m, 2] * ends[2]
            out = out - arr[m]
            fwd[m] += pick(gbt[...], out)
            bwd[m] += pick(gft[...], out)

    finish(0, True)

    @pl.loop(1, STEPS)
    def _(step):
        gather_send(step)
        finish(step)

    wait(imp_all, devs - 1, imp_sem.at[0])

    @pl.loop(0, STEPS)
    def _(step):
        wait(h_send.at[step], total - 1, send_sem.at[0, step])

        @pl.when(dev < owners)
        def _():
            wait(e_send.at[step], owners - 1, send_sem.at[1, step])
            wait(e_recv.at[step], devs - 1, send_sem.at[2, step])

        @pl.when(dev >= owners)
        def _():
            wait(e_send.at[step], owners, send_sem.at[1, step])

        wait(v_send.at[step], total - 1, send_sem.at[3, step])


def on_device(
    areas,
    devs,
    wave_fwd,
    wave_bwd,
    seg_reflect,
    seg_count,
    modal_admit,
    modal_transform,
    end_slot,
    recv_bus,
    bus_impedance,
    link_bus,
    link_resist,
    source_current,
):
    total = areas * devs
    cases, segs = wave_fwd.shape[2], wave_fwd.shape[1]
    cap = recv_bus.shape[1] // total
    rows = -(-cap // 8) * 8
    if rows != cap:
        end_slot = end_slot // cap * rows + end_slot % cap
        recv_bus = jnp.pad(
            recv_bus.reshape(total, cap), ((0, 0), (0, rows - cap)), constant_values=-1
        ).reshape(1, total * rows)
    slots = total * rows
    buses = bus_impedance.shape[2]
    links = link_bus.shape[0]
    vmem = pl.BlockSpec(memory_space=pltpu.VMEM)
    smem = pl.BlockSpec(memory_space=pltpu.SMEM)
    wide = 3 * cases
    volts, fwd, bwd = pl.pallas_call(
        functools.partial(kernel, areas, devs),
        out_shape=(
            jax.ShapeDtypeStruct((STEPS, 3, buses, cases), F32),
            jax.ShapeDtypeStruct(wave_fwd.shape, F32),
            jax.ShapeDtypeStruct(wave_bwd.shape, F32),
        ),
        in_specs=[vmem] * 5 + [smem] + [vmem] * 6,
        out_specs=(vmem, vmem, vmem),
        scratch_shapes=[
            pltpu.VMEM((STEPS, total, rows, wide), F32),
            pltpu.VMEM((STEPS, total, rows, wide), F32),
            pltpu.VMEM((STEPS, links // 8, 8, wide), F32),
            pltpu.VMEM((STEPS, devs, 8, wide), F32),
            pltpu.VMEM((STEPS, links // 8, 8, wide), F32),
            pltpu.VMEM((STEPS, total, rows, wide), F32),
            pltpu.VMEM((STEPS, total, rows, wide), F32),
            pltpu.VMEM((devs, 3, 3, buses), F32),
            pltpu.VMEM((slots, segs), BF16),
            pltpu.VMEM((slots, segs), BF16),
            pltpu.VMEM((segs, slots), BF16),
            pltpu.VMEM((segs, slots), BF16),
            pltpu.VMEM((buses, slots), BF16),
            pltpu.VMEM((slots, buses), BF16),
            pltpu.VMEM((links, buses), BF16),
            pltpu.VMEM((buses, links), BF16),
            pltpu.VMEM((3, slots, cases), F32),
            pltpu.VMEM((9, buses, cases), F32),
            pltpu.VMEM((3, segs, cases), F32),
            pltpu.VMEM((3, segs, cases), F32),
            pltpu.VMEM((3, segs, cases), F32),
            pltpu.VMEM((3, segs, cases), F32),
            pltpu.VMEM((3, slots, cases), F32),
            pltpu.VMEM((3, buses, cases), F32),
            pltpu.VMEM((3 * links, 3 * links), F32),
            pltpu.SemaphoreType.DMA((4, STEPS)),
            pltpu.SemaphoreType.DMA((4, STEPS)),
            pltpu.SemaphoreType.DMA((2,)),
        ],
        compiler_params=pltpu.CompilerParams(
            collective_id=0, has_side_effects=True, vmem_limit_bytes=60 * 1024 * 1024
        ),
        name="transient",
    )(
        wave_fwd,
        wave_bwd,
        seg_reflect,
        seg_count,
        modal_admit,
        modal_transform,
        end_slot.T,
        recv_bus,
        bus_impedance,
        link_bus.T,
        link_resist.reshape(1, links),
        jnp.transpose(source_current, (0, 2, 1, 3)),
    )
    return (jnp.transpose(volts, (0, 2, 1, 3)), fwd, bwd)


def solution(mesh):
    in_specs = (
        P(None, ("area", "dev"), None),
        P(None, ("area", "dev"), None),
        P(None, ("area", "dev")),
        P(("area", "dev"), None),
        P(None, ("area", "dev")),
        P(),
        P(("area", "dev"), None),
        P(("area", "dev"), None),
        P(None, None, ("area", "dev")),
        P("area", None),
        P("area"),
        P(None, ("area", "dev"), None, None),
    )
    out_specs = (
        P(None, ("area", "dev"), None, None),
        P(None, ("area", "dev"), None),
        P(None, ("area", "dev"), None),
    )
    return jax.shard_map(
        functools.partial(on_device, mesh.shape["area"], mesh.shape["dev"]),
        mesh=mesh,
        in_specs=in_specs,
        out_specs=out_specs,
        check_vma=False,
    )
```

profile of v0, /device:TPU:0, one launch (start us, length us, event | category | flops | bytes accessed | tf_op | source)
XLA Modules:
  0.0 134.1 jit_solution(8514569472555932513)
XLA Ops:
  0.6 129.3 %transient.1 = (f32[4,3,64,128]{3,2,1,0:T(8,128)}, f32[3,512,128]{2,1,0:T(8,128)}, f32[3,512,128]{2,1,0:T(8,128)}) custom-call(f32[3,512,128]{2,1,0:T(8,128)} %fwd_in.1, f32[3,512,128]{2,1,0:T(8,128)} %bwd_in.1, f32[3,512]{1,0:T(4,128)} %refl_ref.1, s32[1,64]{1,0:T(1,128)} %count_ref.1, f32[3,64]{1,0:T(4,128)} %admit_ref.1, f32[3,3]{1,0:T(4,128)} %trans_ref.1, ...), custom_call_target="tpu_custom_call" | custom-call | tf_op jit(solution)/shard_map/transient/pallas_call | solution.py:433
  129.9 0.0 copy-start.1
  129.9 1.8 %copy.18 = f32[4,64,3,128]{3,1,2,0:T(8,128)} copy(f32[4,64,3,128]{3,1,2,0:T(8,128)} %bitcast.5) | data formatting | bytes 786432
  131.8 0.0 copy-done.1
  131.8 0.0 copy-start
  131.8 0.9 copy.19
  132.7 0.5 copy-done
  133.2 0.9 copy.20
Async XLA Ops:
  129.9 1.9 %copy-start.1 = (f32[3,512,128]{2,1,0:T(8,128)S(1)}, f32[3,512,128]{2,1,0:T(8,128)}, u32[]{:S(2)}) copy-start(f32[3,512,128]{2,1,0:T(8,128)} %get-tuple-element.13) | copy-start | bytes 2359300
  131.8 1.4 %copy-start = (f32[3,512,128]{2,1,0:T(8,128)S(1)}, f32[3,512,128]{2,1,0:T(8,128)}, u32[]{:S(2)}) copy-start(f32[3,512,128]{2,1,0:T(8,128)} %get-tuple-element.14) | copy-start | bytes 2359300
where the time goes:
time: 136 us; the launch traced here: 134 us
  Pallas kernels  129 us (95%)
  local copies, waits for them, and re-layouts  4.14 us (3%)
    pallas_call x1, Pallas kernels, on_device(): pl.pallas_call(functools.partial(kernel, areas, devs), out_shape=(jax.Sha...  129 us
    unnamed x7, local copies, waits for them, and re-layouts  4.14 us

commit v1 on v0

v1 whole, which is shorter than its diff:
```python
import functools

import jax
import jax.numpy as jnp
from jax import lax
from jax.experimental import pallas as pl
from jax.experimental.pallas import tpu as pltpu
from jax.sharding import PartitionSpec as P

STEPS = 4
HALVES = 2
MESH = pl.DeviceIdType.MESH
F32 = jnp.float32
BF16 = jnp.bfloat16
EXACT = lax.Precision.HIGHEST


def iota(shape, dim):
    return lax.broadcasted_iota(jnp.int32, shape, dim)


def to_column(row):
    n = row.shape[1]
    eye = iota((n, n), 0) == iota((n, n), 1)
    return jnp.sum(jnp.where(eye, row, 0.0), axis=1, keepdims=True)


def to_row(column):
    n = column.shape[0]
    eye = iota((n, n), 0) == iota((n, n), 1)
    return jnp.sum(jnp.where(eye, column, 0.0), axis=0, keepdims=True)


def onehot(flag):
    return jnp.where(flag, 1.0, 0.0).astype(BF16)


def high_low(value):
    high = value.astype(BF16)
    return high, (value - high.astype(F32)).astype(BF16)


def pick(matrix, value):
    n = value.shape[1]
    both = jnp.dot(
        matrix, jnp.concatenate(high_low(value), axis=1), preferred_element_type=F32
    )
    return both[:, :n] + both[:, n:]


def swap(value):
    return pltpu.roll(value, value.shape[1] // 2, 1)


def lower(value):
    return iota(value.shape, 1) < value.shape[1] // 2


def pack(value):
    n = value.shape[0] // 2
    top, bottom = value[:n], value[n:]
    left = lower(top)
    return jnp.where(left, top, swap(bottom)), jnp.where(left, swap(top), bottom)


def unpack(first, second):
    left = lower(first)
    return jnp.concatenate(
        [jnp.where(left, first, swap(second)), jnp.where(left, swap(first), second)], axis=0
    )


def fold(result):
    m = result.shape[0] // 4
    tl, tr, bl, br = (result[k * m : (k + 1) * m] for k in range(4))
    left = lower(tl)
    return jnp.where(left, tl, br) + swap(jnp.where(left, bl, tr))


def packed_dot(table, parts):
    n = parts[0].shape[1]
    both = jnp.concatenate(high_low(jnp.concatenate(parts, axis=1)), axis=0)
    result = jnp.dot(table, both, preferred_element_type=F32)
    return [fold(result[:, k * n : (k + 1) * n]) for k in range(len(parts))]


def kernel(
    areas,
    devs,
    fwd_in,
    bwd_in,
    refl_ref,
    count_ref,
    admit_ref,
    trans_ref,
    slot_ref,
    recv_ref,
    imp_ref,
    link_ref,
    resist_ref,
    src_in,
    volt_out,
    fwd_out,
    bwd_out,
    fwd,
    bwd,
    src,
    volt,
    h_send,
    h_recv,
    e_recv,
    v_send,
    v_recv,
    imp_all,
    zrow,
    ends_of,
    swap_of,
    gbt,
    gft,
    rsum,
    rback,
    ct,
    u,
    adm,
    zpack,
    spack,
    keep_f,
    take_f,
    keep_b,
    take_b,
    arr,
    nxt,
    out,
    open_volts,
    minv,
    send_sem,
    recv_sem,
    imp_sem,
    in_sem,
    out_sem,
):
    total = areas * devs
    area, dev = lax.axis_index("area"), lax.axis_index("dev")
    me = area * devs + dev
    cases = fwd.shape[2]
    segs = fwd.shape[1]
    lines = slot_ref.shape[1]
    slots = recv_ref.shape[1]
    buses = imp_ref.shape[2]
    links = link_ref.shape[1]
    rows = slots // total
    few = rows // 2
    packed = slots // 2
    near = buses // 2
    some = links // 2

    inputs = [
        pltpu.make_async_copy(a, b, in_sem.at[k])
        for k, (a, b) in enumerate(((fwd_in, fwd), (bwd_in, bwd), (src_in, src)))
    ]
    for copy in inputs:
        copy.start()

    barrier = pltpu.get_barrier_semaphore()

    def peer_of(p):
        peer = lax.rem(me + p, total)
        return peer, (peer // devs, lax.rem(peer, devs))

    @pl.loop(1, total)
    def _(p):
        _, where = peer_of(p)
        pl.semaphore_signal(barrier, inc=1, device_id=where, device_id_type=MESH)

    def push_all(send, recv, phase, step, h):
        @pl.loop(1, total, unroll=total <= 32)
        def _(p):
            peer, where = peer_of(p)
            pltpu.make_async_remote_copy(
                src_ref=send.at[step, h, peer],
                dst_ref=recv.at[step, h, me],
                send_sem=send_sem.at[phase, step, h],
                recv_sem=recv_sem.at[phase, step, h],
                device_id=where,
                device_id_type=MESH,
            ).start()

        recv[step, h, me] = send[step, h, me]

    def wait(buf, count, sem):
        ref = buf.at[pl.ds(0, count)]
        pltpu.make_async_copy(ref, ref, sem).wait()

    def place(slot):
        bits = few.bit_length() - 1
        upper = lax.shift_right_logical(slot, bits)
        return (upper & 1) * packed + lax.shift_right_logical(upper, 1) * few + (slot & (few - 1))

    counts_row = count_ref[...].astype(F32)
    counts_col = to_column(counts_row)
    square = (lines, lines)
    first_col = jnp.sum(
        jnp.where(iota(square, 1) < iota(square, 0), counts_row, 0.0), axis=1, keepdims=True
    )
    last_col = first_col + counts_col - 1.0
    slot0_row = place(slot_ref[0:1, :]).astype(F32)
    slot1_row = place(slot_ref[1:2, :]).astype(F32)
    seg_lane = iota((lines, segs), 1).astype(F32)
    slot_sub = iota((slots, lines), 0).astype(F32)
    q0, q1 = onehot(slot_sub == slot0_row), onehot(slot_sub == slot1_row)
    ends_of[:, :segs] = jnp.dot(
        q0, onehot(seg_lane == first_col), preferred_element_type=F32
    ).astype(BF16)
    ends_of[:, segs:] = jnp.dot(
        q1, onehot(seg_lane == last_col), preferred_element_type=F32
    ).astype(BF16)
    held = q0.astype(F32) + q1.astype(F32)
    for m in range(3):
        column = 2.0 * jnp.sum(held * admit_ref[m : m + 1, :], axis=1, keepdims=True)
        wide = jnp.broadcast_to(column, (slots, cases))
        adm[m] = jnp.where(lower(wide[:packed]), wide[:packed], wide[packed:])

    def gather(target):
        for m in range(3):
            both = jnp.concatenate([bwd[m], fwd[m]], axis=0)
            for h, half in enumerate(pack(pick(ends_of[...], both))):
                target[h, m] = half

    def inject(step, h):
        for i in range(3):
            value = trans_ref[0, i] * (adm[0] * arr[h, 0])
            value = value + trans_ref[1, i] * (adm[1] * arr[h, 1])
            value = value + trans_ref[2, i] * (adm[2] * arr[h, 2])
            h_send[step, h, :, i] = value.reshape(total, few, cases)

    inputs[0].wait()
    inputs[1].wait()
    gather(arr)
    for h in range(HALVES):
        inject(0, h)
    pl.semaphore_wait(barrier, total - 1)

    @pl.loop(1, devs)
    def _(p):
        other = lax.rem(dev + p, devs)
        pltpu.make_async_remote_copy(
            src_ref=imp_ref,
            dst_ref=imp_all.at[dev],
            send_sem=imp_sem.at[0],
            recv_sem=imp_sem.at[1],
            device_id=(area, other),
            device_id_type=MESH,
        ).start()

    for h in range(HALVES):
        push_all(h_send, h_recv, 0, 0, h)
    imp_all[dev] = imp_ref[...]

    recv_placed = jnp.where(
        iota((slots, slots), 0) == place(iota((slots, slots), 1)), recv_ref[...].astype(F32), 0.0
    )
    recv_col = jnp.sum(recv_placed, axis=1, keepdims=True)
    recv_row = to_row(recv_col)
    for k in range(4):
        side = slice((k % 2) * packed, (k % 2 + 1) * packed)
        bus = (iota((near, packed), 0) + (k // 2) * near).astype(F32)
        block = onehot(bus == recv_row[:, side])
        for w in range(2):
            rsum[k * near : (k + 1) * near, w * packed : (w + 1) * packed] = block
        side = slice((k // 2) * packed, (k // 2 + 1) * packed)
        bus = ((iota((packed, 2 * near), 1) & (near - 1)) + (k % 2) * near).astype(F32)
        rback[k * packed : (k + 1) * packed, :] = onehot(bus == recv_col[side])

    link0_row, link1_row = link_ref[0:1, :].astype(F32), link_ref[1:2, :].astype(F32)
    link0, link1 = to_column(link0_row), to_column(link1_row)

    def incidence(index, a, b):
        index = index.astype(F32)
        return jnp.where(index == a, 1.0, 0.0) - jnp.where(index == b, 1.0, 0.0)

    blocks = []
    for k in range(4):
        side = slice((k // 2) * some, (k // 2 + 1) * some)
        bus = (iota((some, 2 * near), 1) & (near - 1)) + (k % 2) * near + dev * buses
        blocks.append(incidence(bus, link0[side], link1[side]))
    ct[...] = jnp.concatenate(blocks, axis=0).astype(BF16)
    zcols = [to_column(imp_ref[ij // 3, ij % 3 : ij % 3 + 1, :]) for ij in range(9)]
    for ij in range(9):
        wide = jnp.broadcast_to(zcols[ij], (buses, cases))
        zpack[ij] = jnp.where(lower(wide[:near]), wide[:near], wide[near:])
    inputs[2].wait()

    @pl.loop(0, STEPS)
    def _(step):
        for i in range(3):
            for h, half in enumerate(pack(src[step, i])):
                spack[step, h, i] = half

    def wave_tables():
        first_row, last_row = to_row(first_col), to_row(last_col)
        slot0_col, slot1_col = to_column(slot0_row), to_column(slot1_row)
        seg_sub = iota((segs, lines), 0).astype(F32)
        slot_lane = iota((lines, slots), 1).astype(F32)
        fst = onehot(seg_sub == first_row)
        lst = onehot(seg_sub == last_row)
        gbt[...] = jnp.dot(
            fst, onehot(slot_lane == slot0_col), preferred_element_type=F32
        ).astype(BF16)
        gft[...] = jnp.dot(
            lst, onehot(slot_lane == slot1_col), preferred_element_type=F32
        ).astype(BF16)
        not_first = 1.0 - jnp.sum(fst.astype(F32), axis=1, keepdims=True)
        not_last = 1.0 - jnp.sum(lst.astype(F32), axis=1, keepdims=True)
        for m in range(3):
            r = to_column(refl_ref[m : m + 1, :])
            r_next = pltpu.roll(jnp.broadcast_to(r, (segs, cases)), segs - 1, 0)
            keep_f[m] = jnp.broadcast_to((1.0 - r) * not_first, (segs, cases))
            take_f[m] = jnp.broadcast_to(r * not_first, (segs, cases))
            keep_b[m] = (1.0 - r_next) * not_last
            take_b[m] = r_next * not_last
        single = jnp.where(counts_row == 1.0, 1.0, 0.0)
        a, b = q0.astype(F32) * single, q1.astype(F32) * single
        across = (((1,), (1,)), ((), ()))
        swaps = lax.dot_general(a.astype(BF16), q1, across, preferred_element_type=F32)
        swaps = swaps + lax.dot_general(b.astype(BF16), q0, across, preferred_element_type=F32)
        swaps = swaps.astype(BF16)
        for k in range(4):
            block = swaps[
                (k // 2) * packed : (k // 2 + 1) * packed, (k % 2) * packed : (k % 2 + 1) * packed
            ]
            for w in range(2):
                swap_of[k * packed : (k + 1) * packed, w * packed : (w + 1) * packed] = block

    def advance():
        for m in range(3):
            f, b = fwd[m], bwd[m]
            fwd[m] = keep_f[m] * pltpu.roll(f, 1, 0) + take_f[m] * b
            bwd[m] = keep_b[m] * pltpu.roll(b, segs - 1, 0) + take_b[m] * f

    def scatter(m):
        value = unpack(out[0, m], out[1, m])
        fwd[m] += pick(gbt[...], value)
        bwd[m] += pick(gft[...], value)

    def form_links():
        wait(imp_all, devs - 1, imp_sem.at[1])
        for d in range(devs):
            for i in range(3):
                zrow[3 * i : 3 * i + 3, d * buses : (d + 1) * buses] = imp_all[d, i]
        c = incidence(iota((links, devs * buses), 1), link0, link1)
        c_exact = c.astype(BF16)
        eye = iota((links, links), 0) == iota((links, links), 1)
        for i in range(3):
            for j in range(i + 1):
                z = zrow[3 * i + j : 3 * i + j + 1, :]
                high = z.astype(BF16).astype(F32)
                mid = (z - high).astype(BF16).astype(F32)
                terms = jnp.concatenate([c * high, c * mid, c * (z - high - mid)], axis=0)
                terms = lax.dot_general(
                    terms.astype(BF16), c_exact, (((1,), (1,)), ((), ())), preferred_element_type=F32
                )
                block = terms[:links] + terms[links : 2 * links] + terms[2 * links :]
                here = slice(i * links, (i + 1) * links)
                past = slice(j * links, (j + 1) * links)
                if i == j:
                    block = block + jnp.where(eye, resist_ref[...], 0.0)
                else:
                    minv[past, here] = block
                minv[here, past] = block

    order = 3 * links
    lane = iota((order, order), 1)

    def eliminate(start, stop):
        @pl.loop(start, stop)
        def _(n):
            spots = [n + w * links for w in range(3)]
            a = minv[...]
            lines_ = [minv[pl.ds(k, 1), :] for k in spots]
            here = [lane == k for k in spots]
            edge = [lane[:1] == k for k in spots]
            cols = [jnp.sum(jnp.where(g, a, 0.0), axis=1, keepdims=True) for g in here]
            block = [
                [jnp.sum(jnp.where(g, r, 0.0), axis=1, keepdims=True) for g in edge]
                for r in lines_
            ]
            for v in range(3):
                inverse = 1.0 / block[v][v]
                row, col = lines_[v], cols[v] * inverse
                a = a - col * row
                scaled = row * inverse
                factor = [block[w][v] for w in range(3)]
                across = [block[v][w] * inverse for w in range(3)]
                for w in range(3):
                    lines_[w] = scaled if w == v else lines_[w] - factor[w] * scaled
                    cols[w] = col if w == v else cols[w] - block[v][w] * col
                for w in range(3):
                    for x in range(3):
                        if w != v and x != v:
                            block[w][x] = block[w][x] - factor[w] * across[x]
                for w in range(3):
                    if w != v:
                        block[w][v], block[v][w] = factor[w] * inverse, across[w]
                block[v][v] = -inverse
            for w in range(3):
                a = jnp.where(here[w], cols[w], a)
                for x in range(3):
                    lines_[w] = jnp.where(edge[x], block[w][x], lines_[w])
            minv[...] = a
            for w in range(3):
                minv[pl.ds(spots[w], 1), :] = lines_[w]

    def link_effect():
        source, target = iota((order, 2 * cases), 0), iota((order, 2 * cases), 1)
        side, spot = target // cases, target % cases
        wanted = (spot // some) * links + side * some + spot % some
        chosen = jnp.where((source == wanted) & (spot < 3 * some), 1.0, 0.0)
        inverse = jnp.dot(minv[...], chosen, precision=EXACT, preferred_element_type=F32)
        c = incidence(iota((buses, links), 0) + dev * buses, link0_row, link1_row)
        drops = [
            jnp.dot(
                c,
                inverse[k * links : (k + 1) * links],
                precision=EXACT,
                preferred_element_type=F32,
            )
            for k in range(3)
        ]
        for i in range(3):
            effect = zcols[3 * i] * drops[0] + zcols[3 * i + 1] * drops[1]
            effect = effect + zcols[3 * i + 2] * drops[2]
            for w, part in enumerate(high_low(effect)):
                for k in range(4):
                    spot = (4 * w + k) * 3 * near + i * near
                    u[spot : spot + near, :] = part[
                        (k // 2) * near : (k // 2 + 1) * near,
                        (k % 2) * cases : (k % 2) * cases + 3 * some,
                    ]

    def apply(values):
        return [
            zpack[3 * i] * values[0] + zpack[3 * i + 1] * values[1] + zpack[3 * i + 2] * values[2]
            for i in range(3)
        ]

    def share(step, h):
        wait(h_recv.at[step, h], total - 1, recv_sem.at[0, step, h])
        parts = [h_recv[step, h, :, i].reshape(packed, cases) for i in range(3)]
        total_in = packed_dot(rsum[...], parts)
        volts = apply([spack[step, h, i] + total_in[i] for i in range(3)])
        for i in range(3):
            open_volts[h, i] = volts[i]
        opened = packed_dot(ct[...], volts)
        for i in range(3):
            e_recv[step, h, dev, i * some : (i + 1) * some, :] = opened[i]

        @pl.loop(1, devs, unroll=devs <= 8)
        def _(p):
            pltpu.make_async_remote_copy(
                src_ref=e_recv.at[step, h, dev],
                dst_ref=e_recv.at[step, h, dev],
                send_sem=send_sem.at[1, step, h],
                recv_sem=recv_sem.at[1, step, h],
                device_id=(area, lax.rem(dev + p, devs)),
                device_id_type=MESH,
            ).start()

    def settle(step, h):
        wait(e_recv.at[step, h], devs - 1, recv_sem.at[1, step, h])
        opened = jnp.sum(e_recv[step, h], axis=0)
        result = jnp.dot(
            u[...], jnp.concatenate(high_low(opened), axis=1), preferred_element_type=F32
        )
        main = 12 * near
        change = fold(result[:main, :cases] + result[:main, cases:] + result[main:, :cases])
        volts = [open_volts[h, i] + change[i * near : (i + 1) * near] for i in range(3)]
        half = cases // 2
        mine = slice(h * half, (h + 1) * half)
        for i in range(3):
            turned = swap(volts[i])
            low, high = (volts[i], turned) if h == 0 else (turned, volts[i])
            volt[step, i, :near, mine] = low[:, mine]
            volt[step, i, near:, mine] = high[:, mine]
        sent = packed_dot(rback[...], volts)
        for i in range(3):
            v_send[step, h, :, i] = sent[i].reshape(total, few, cases)
        push_all(v_send, v_recv, 2, step, h)

    def leave(step, h):
        wait(v_recv.at[step, h], total - 1, recv_sem.at[2, step, h])
        ends = [v_recv[step, h, :, i].reshape(packed, cases) for i in range(3)]
        results = []
        for m in range(3):
            value = trans_ref[m, 0] * ends[0] + trans_ref[m, 1] * ends[1] + trans_ref[m, 2] * ends[2]
            value = value - arr[h, m]
            out[h, m] = value
            results.append(value)
        return results

    def volt_copy(step):
        return pltpu.make_async_copy(volt.at[step], volt_out.at[step], out_sem.at[step])

    form_links()
    eliminate(0, links // 4)
    for h in range(HALVES):
        share(0, h)
    eliminate(links // 4, links)
    link_effect()
    for h in range(HALVES):
        settle(0, h)
    volt_copy(0).start()
    wave_tables()
    advance()
    gather(nxt)

    @pl.loop(1, STEPS)
    def _(step):
        for h in range(HALVES):
            moved = packed_dot(swap_of[...], leave(step - 1, h))
            for m in range(3):
                arr[h, m] = nxt[h, m] + moved[m]
            inject(step, h)
            push_all(h_send, h_recv, 0, step, h)
        for m in range(3):
            scatter(m)
        advance()

        @pl.when(step < STEPS - 1)
        def _():
            gather(nxt)

        for h in range(HALVES):
            share(step, h)
        for h in range(HALVES):
            settle(step, h)
        volt_copy(step).start()

    for h in range(HALVES):
        leave(STEPS - 1, h)
    outputs = []
    for m in range(3):
        scatter(m)
        for k, (a, b) in enumerate(((fwd, fwd_out), (bwd, bwd_out))):
            outputs.append(
                pltpu.make_async_copy(a.at[m], b.at[m], out_sem.at[STEPS + 2 * m + k])
            )
            outputs[-1].start()

    wait(imp_all, devs - 1, imp_sem.at[0])

    @pl.loop(0, STEPS)
    def _(step):
        volt_copy(step).wait()
        for h in range(HALVES):
            wait(h_send.at[step, h], total - 1, send_sem.at[0, step, h])
            wait(e_recv.at[step, h], devs - 1, send_sem.at[1, step, h])
            wait(v_send.at[step, h], total - 1, send_sem.at[2, step, h])

    for copy in outputs:
        copy.wait()


def hand_over(volt_in, fwd_in, bwd_in, volt_out, fwd_out, bwd_out, volt, fwd, bwd, sems):
    groups = ((fwd_in, fwd, fwd_out), (bwd_in, bwd, bwd_out), (volt_in, volt, volt_out))
    copies = [
        (
            pltpu.make_async_copy(a.at[n], b.at[n], sems.at[0, k, n]),
            pltpu.make_async_copy(b.at[n], c.at[n], sems.at[1, k, n]),
        )
        for k, (a, b, c) in enumerate(groups)
        for n in range(a.shape[0])
    ]
    for first, _ in copies:
        first.start()
    for first, second in copies:
        first.wait()
        second.start()
    for _, second in copies:
        second.wait()


def on_device(
    areas,
    devs,
    wave_fwd,
    wave_bwd,
    seg_reflect,
    seg_count,
    modal_admit,
    modal_transform,
    end_slot,
    recv_bus,
    bus_impedance,
    link_bus,
    link_resist,
    source_current,
):
    total = areas * devs
    cases, segs = wave_fwd.shape[2], wave_fwd.shape[1]
    cap = recv_bus.shape[1] // total
    rows = -(-cap // 8) * 8
    if rows != cap:
        end_slot = end_slot // cap * rows + end_slot % cap
        recv_bus = jnp.pad(
            recv_bus.reshape(total, cap), ((0, 0), (0, rows - cap)), constant_values=-1
        ).reshape(1, total * rows)
    slots = total * rows
    buses = bus_impedance.shape[2]
    links = link_bus.shape[0]
    vmem = pl.BlockSpec(memory_space=pltpu.VMEM)
    smem = pl.BlockSpec(memory_space=pltpu.SMEM)
    anywhere = pl.BlockSpec(memory_space=pl.ANY)
    volt_shape = (STEPS, 3, buses, cases)
    sent = (STEPS, HALVES, total, 3, rows // 2, cases)
    half_slots = (HALVES, 3, slots // 2, cases)
    results = pl.pallas_call(
        functools.partial(kernel, areas, devs),
        out_shape=(
            jax.ShapeDtypeStruct(volt_shape, F32),
            jax.ShapeDtypeStruct(wave_fwd.shape, F32),
            jax.ShapeDtypeStruct(wave_bwd.shape, F32),
        ),
        in_specs=[anywhere] * 2 + [vmem] * 3 + [smem] + [vmem] * 5 + [anywhere],
        out_specs=(anywhere, anywhere, anywhere),
        scratch_shapes=[
            pltpu.VMEM(wave_fwd.shape, F32),
            pltpu.VMEM(wave_bwd.shape, F32),
            pltpu.VMEM(volt_shape, F32),
            pltpu.VMEM(volt_shape, F32),
            pltpu.VMEM(sent, F32),
            pltpu.VMEM(sent, F32),
            pltpu.VMEM((STEPS, HALVES, devs, 3 * links // 2, cases), F32),
            pltpu.VMEM(sent, F32),
            pltpu.VMEM(sent, F32),
            pltpu.VMEM((devs, 3, 3, buses), F32),
            pltpu.VMEM((16, devs * buses), F32),
            pltpu.VMEM((slots, 2 * segs), BF16),
            pltpu.VMEM((2 * slots, slots), BF16),
            pltpu.VMEM((segs, slots), BF16),
            pltpu.VMEM((segs, slots), BF16),
            pltpu.VMEM((2 * buses, slots), BF16),
            pltpu.VMEM((2 * slots, buses), BF16),
            pltpu.VMEM((2 * links, buses), BF16),
            pltpu.VMEM((12 * buses, 3 * links // 2), BF16),
            pltpu.VMEM((3, slots // 2, cases), F32),
            pltpu.VMEM((9, buses // 2, cases), F32),
            pltpu.VMEM((STEPS, HALVES, 3, buses // 2, cases), F32),
            pltpu.VMEM((3, segs, cases), F32),
            pltpu.VMEM((3, segs, cases), F32),
            pltpu.VMEM((3, segs, cases), F32),
            pltpu.VMEM((3, segs, cases), F32),
            pltpu.VMEM(half_slots, F32),
            pltpu.VMEM(half_slots, F32),
            pltpu.VMEM(half_slots, F32),
            pltpu.VMEM((HALVES, 3, buses // 2, cases), F32),
            pltpu.VMEM((3 * links, 3 * links), F32),
            pltpu.SemaphoreType.DMA((3, STEPS, HALVES)),
            pltpu.SemaphoreType.DMA((3, STEPS, HALVES)),
            pltpu.SemaphoreType.DMA((2,)),
            pltpu.SemaphoreType.DMA((3,)),
            pltpu.SemaphoreType.DMA((STEPS + 6,)),
        ],
        compiler_params=pltpu.CompilerParams(
            collective_id=0, has_side_effects=True, vmem_limit_bytes=60 * 1024 * 1024
        ),
        name="transient",
    )(
        wave_fwd,
        wave_bwd,
        seg_reflect,
        seg_count,
        modal_admit,
        modal_transform,
        end_slot.T,
        recv_bus,
        bus_impedance,
        link_bus.T,
        link_resist.reshape(1, links),
        jnp.transpose(source_current, (0, 2, 1, 3)),
    )
    volts, fwd, bwd = pl.pallas_call(
        hand_over,
        out_shape=tuple(jax.ShapeDtypeStruct(a.shape, F32) for a in results),
        in_specs=[anywhere] * 3,
        out_specs=(anywhere,) * 3,
        scratch_shapes=[pltpu.VMEM(a.shape, F32) for a in results]
        + [pltpu.SemaphoreType.DMA((2, 3, STEPS))],
        name="hand_over",
    )(*results)
    return (jnp.transpose(volts, (0, 2, 1, 3)), fwd, bwd)


def solution(mesh):
    in_specs = (
        P(None, ("area", "dev"), None),
        P(None, ("area", "dev"), None),
        P(None, ("area", "dev")),
        P(("area", "dev"), None),
        P(None, ("area", "dev")),
        P(),
        P(("area", "dev"), None),
        P(("area", "dev"), None),
        P(None, None, ("area", "dev")),
        P("area", None),
        P("area"),
        P(None, ("area", "dev"), None, None),
    )
    out_specs = (
        P(None, ("area", "dev"), None, None),
        P(None, ("area", "dev"), None),
        P(None, ("area", "dev"), None),
    )
    return jax.shard_map(
        functools.partial(on_device, mesh.shape["area"], mesh.shape["dev"]),
        mesh=mesh,
        in_specs=in_specs,
        out_specs=out_specs,
        check_vma=False,
    )
```

time: 136 us -> 112 us (0.82); the launches traced: 134 us -> 112 us
  Pallas kernels: 129 us -> 111 us
  local copies, waits for them, and re-layouts: 4.14 us -> 0 us
    pallas_call x1, Pallas kernels: 129 us -> 109 us  [on_device(): pl.pallas_call(functools.partial(kernel, areas, devs), out_shape=(jax.Sha...]
    unnamed x7 -> x0, local copies, waits for them, and re-layouts: 4.14 us -> none
    pallas_call x0 -> x1, Pallas kernels: none -> 2.42 us  [on_device(): pl.pallas_call(hand_over, out_shape=tuple((jax.ShapeDtypeStruct(a.shape,...]
where the time goes in v1:
time: 112 us
  Pallas kernels  111 us (99%)
    pallas_call x1, Pallas kernels, on_device(): pl.pallas_call(functools.partial(kernel, areas, devs), out_shape=(jax.Sha...  109 us
    pallas_call x1, Pallas kernels, on_device(): pl.pallas_call(hand_over, out_shape=tuple((jax.ShapeDtypeStruct(a.shape,...  2.42 us

profile of v1, /device:TPU:0, one launch (start us, length us, event | category | flops | bytes accessed | tf_op | source)
XLA Modules:
  0.0 112.1 jit_solution(14020380042628589116)
XLA Ops:
  0.6 109.1 %transient.1 = (f32[4,3,64,128]{3,2,1,0:T(8,128)}, f32[3,512,128]{2,1,0:T(8,128)}, f32[3,512,128]{2,1,0:T(8,128)}) custom-call(f32[3,512,128]{2,1,0:T(8,128)} %fwd_in.1, f32[3,512,128]{2,1,0:T(8,128)} %bwd_in.1, f32[3,512]{1,0:T(4,128)} %refl_ref.1, s32[1,64]{1,0:T(1,128)} %count_ref.1, f32[3,64]{1,0:T(4,128)} %admit_ref.1, f32[3,3]{1,0:T(4,128)} %trans_ref.1, ...), custom_call_target="tpu_custom_call" | custom-call | tf_op jit(solution)/shard_map/transient/pallas_call | solution.py:616
  109.7 2.4 %hand_over.1 = (f32[4,3,64,128]{3,2,1,0:T(8,128)}, f32[3,512,128]{2,1,0:T(8,128)}, f32[3,512,128]{2,1,0:T(8,128)}) custom-call(f32[4,3,64,128]{3,2,1,0:T(8,128)} %get-tuple-element.9.volt_in, f32[3,512,128]{2,1,0:T(8,128)} %get-tuple-element.10.fwd_in, f32[3,512,128]{2,1,0:T(8,128)} %get-tuple-element.11.bwd_in), custom_call_target="tpu_custom_call" | custom-call | tf_op jit(solution)/shard_map/hand_over/pallas_call | solution.py:681

commit v2 on v1

--- a/solution.py
+++ b/solution.py
@@ -132,7 +132,12 @@
     nxt,
     out,
     open_volts,
-    minv,
+    near_inv,
+    cross,
+    cross_back,
+    far_inv,
+    ahead,
+    inverse,
     send_sem,
     recv_sem,
     imp_sem,
@@ -164,16 +169,17 @@
     barrier = pltpu.get_barrier_semaphore()
 
     def peer_of(p):
-        peer = lax.rem(me + p, total)
-        return peer, (peer // devs, lax.rem(peer, devs))
-
-    @pl.loop(1, total)
+        other_area = area ^ (areas - 1 - lax.rem(p, areas))
+        other_dev = dev ^ (devs - 1 - p // areas)
+        return other_area * devs + other_dev, (other_area, other_dev)
+
+    @pl.loop(0, total - 1)
     def _(p):
         _, where = peer_of(p)
         pl.semaphore_signal(barrier, inc=1, device_id=where, device_id_type=MESH)
 
     def push_all(send, recv, phase, step, h):
-        @pl.loop(1, total, unroll=total <= 32)
+        @pl.loop(0, total - 1, unroll=total <= 32)
         def _(p):
             peer, where = peer_of(p)
             pltpu.make_async_remote_copy(
@@ -360,21 +366,22 @@
                     terms.astype(BF16), c_exact, (((1,), (1,)), ((), ())), preferred_element_type=F32
                 )
                 block = terms[:links] + terms[links : 2 * links] + terms[2 * links :]
-                here = slice(i * links, (i + 1) * links)
-                past = slice(j * links, (j + 1) * links)
                 if i == j:
                     block = block + jnp.where(eye, resist_ref[...], 0.0)
-                else:
-                    minv[past, here] = block
-                minv[here, past] = block
-
-    order = 3 * links
+                for a, b in ((i, j), (j, i))[: 1 + (i != j)]:
+                    for k, part in enumerate((near_inv, cross, cross_back, far_inv)):
+                        part[a * some : (a + 1) * some, b * some : (b + 1) * some] = block[
+                            (k // 2) * some : (k // 2 + 1) * some,
+                            (k % 2) * some : (k % 2 + 1) * some,
+                        ]
+
+    order = 3 * some
     lane = iota((order, order), 1)
 
-    def eliminate(start, stop):
-        @pl.loop(start, stop)
+    def eliminate(minv):
+        @pl.loop(0, some)
         def _(n):
-            spots = [n + w * links for w in range(3)]
+            spots = [n + w * some for w in range(3)]
             a = minv[...]
             lines_ = [minv[pl.ds(k, 1), :] for k in spots]
             here = [lane == k for k in spots]
@@ -410,22 +417,30 @@
             for w in range(3):
                 minv[pl.ds(spots[w], 1), :] = lines_[w]
 
+    def exact_dot(a, b):
+        return jnp.dot(a, b, precision=EXACT, preferred_element_type=F32)
+
+    def reduce_far():
+        ahead[...] = exact_dot(near_inv[...], cross[...])
+        far_inv[...] += exact_dot(cross_back[...], ahead[...])
+
     def link_effect():
-        source, target = iota((order, 2 * cases), 0), iota((order, 2 * cases), 1)
-        side, spot = target // cases, target % cases
-        wanted = (spot // some) * links + side * some + spot % some
-        chosen = jnp.where((source == wanted) & (spot < 3 * some), 1.0, 0.0)
-        inverse = jnp.dot(minv[...], chosen, precision=EXACT, preferred_element_type=F32)
+        back = exact_dot(cross_back[...], near_inv[...])
+        corner = exact_dot(ahead[...], far_inv[...])
+        parts = (
+            (0, 0, near_inv[...] + exact_dot(corner, back)),
+            (0, 1, corner),
+            (1, 0, exact_dot(far_inv[...], back)),
+            (1, 1, far_inv[...]),
+        )
+        inverse[...] = jnp.zeros_like(inverse)
+        for a, b, part in parts:
+            for k in range(3):
+                inverse[
+                    k, a * some : (a + 1) * some, b * cases : b * cases + 3 * some
+                ] = part[k * some : (k + 1) * some]
         c = incidence(iota((buses, links), 0) + dev * buses, link0_row, link1_row)
-        drops = [
-            jnp.dot(
-                c,
-                inverse[k * links : (k + 1) * links],
-                precision=EXACT,
-                preferred_element_type=F32,
-            )
-            for k in range(3)
-        ]
+        drops = [exact_dot(c, inverse[k]) for k in range(3)]
         for i in range(3):
             effect = zcols[3 * i] * drops[0] + zcols[3 * i + 1] * drops[1]
             effect = effect + zcols[3 * i + 2] * drops[2]
@@ -501,10 +516,11 @@
         return pltpu.make_async_copy(volt.at[step], volt_out.at[step], out_sem.at[step])
 
     form_links()
-    eliminate(0, links // 4)
+    eliminate(near_inv)
     for h in range(HALVES):
         share(0, h)
-    eliminate(links // 4, links)
+    reduce_far()
+    eliminate(far_inv)
     link_effect()
     for h in range(HALVES):
         settle(0, h)
@@ -653,7 +669,8 @@
             pltpu.VMEM(half_slots, F32),
             pltpu.VMEM(half_slots, F32),
             pltpu.VMEM((HALVES, 3, buses // 2, cases), F32),
-            pltpu.VMEM((3 * links, 3 * links), F32),
+            *[pltpu.VMEM((3 * links // 2, 3 * links // 2), F32)] * 5,
+            pltpu.VMEM((3, links, 2 * cases), F32),
             pltpu.SemaphoreType.DMA((3, STEPS, HALVES)),
             pltpu.SemaphoreType.DMA((3, STEPS, HALVES)),
             pltpu.SemaphoreType.DMA((2,)),

time: 112 us -> 108 us (0.964)
  Pallas kernels: 111 us -> 108 us
    pallas_call x1, Pallas kernels: 109 us -> 105 us  [on_device(): pl.pallas_call(functools.partial(kernel, areas, devs), out_shape=(jax.Sha...]
where the time goes in v2:
time: 108 us
  Pallas kernels  108 us (100%)
    pallas_call x1, Pallas kernels, on_device(): pl.pallas_call(functools.partial(kernel, areas, devs), out_shape=(jax.Sha...  105 us
    pallas_call x1, Pallas kernels, on_device(): pl.pallas_call(hand_over, out_shape=tuple((jax.ShapeDtypeStruct(a.shape,...  2.42 us

profile of v2, /device:TPU:0, one launch (start us, length us, event | category | flops | bytes accessed | tf_op | source)
XLA Modules:
  0.0 108.1 jit_solution(16877836508019595009)
XLA Ops:
  0.6 105.1 %transient.1 = (f32[4,3,64,128]{3,2,1,0:T(8,128)}, f32[3,512,128]{2,1,0:T(8,128)}, f32[3,512,128]{2,1,0:T(8,128)}) custom-call(f32[3,512,128]{2,1,0:T(8,128)} %fwd_in.1, f32[3,512,128]{2,1,0:T(8,128)} %bwd_in.1, f32[3,512]{1,0:T(4,128)} %refl_ref.1, s32[1,64]{1,0:T(1,128)} %count_ref.1, f32[3,64]{1,0:T(4,128)} %admit_ref.1, f32[3,3]{1,0:T(4,128)} %trans_ref.1, ...), custom_call_target="tpu_custom_call" | custom-call | tf_op jit(solution)/shard_map/transient/pallas_call | solution.py:632
  105.7 2.4 %hand_over.1 = (f32[4,3,64,128]{3,2,1,0:T(8,128)}, f32[3,512,128]{2,1,0:T(8,128)}, f32[3,512,128]{2,1,0:T(8,128)}) custom-call(f32[4,3,64,128]{3,2,1,0:T(8,128)} %get-tuple-element.9.volt_in, f32[3,512,128]{2,1,0:T(8,128)} %get-tuple-element.10.fwd_in, f32[3,512,128]{2,1,0:T(8,128)} %get-tuple-element.11.bwd_in), custom_call_target="tpu_custom_call" | custom-call | tf_op jit(solution)/shard_map/hand_over/pallas_call | solution.py:698

commit v3 on v2

--- a/solution.py
+++ b/solution.py
@@ -109,6 +109,7 @@
     h_send,
     h_recv,
     e_recv,
+    e_pair,
     v_send,
     v_recv,
     imp_all,
@@ -173,6 +174,10 @@
         other_dev = dev ^ (devs - 1 - p // areas)
         return other_area * devs + other_dev, (other_area, other_dev)
 
+    def turned_of(p):
+        peer = lax.rem(me + p + 1, total)
+        return peer, (peer // devs, lax.rem(peer, devs))
+
     @pl.loop(0, total - 1)
     def _(p):
         _, where = peer_of(p)
@@ -181,7 +186,7 @@
     def push_all(send, recv, phase, step, h):
         @pl.loop(0, total - 1, unroll=total <= 32)
         def _(p):
-            peer, where = peer_of(p)
+            peer, where = turned_of(p) if phase == 2 else peer_of(p)
             pltpu.make_async_remote_copy(
                 src_ref=send.at[step, h, peer],
                 dst_ref=recv.at[step, h, me],
@@ -467,22 +472,34 @@
             open_volts[h, i] = volts[i]
         opened = packed_dot(ct[...], volts)
         for i in range(3):
-            e_recv[step, h, dev, i * some : (i + 1) * some, :] = opened[i]
-
-        @pl.loop(1, devs, unroll=devs <= 8)
+            e_recv[step, h, dev // 2, i * some : (i + 1) * some, :] = opened[i]
+
+        @pl.loop(1, devs // 2, unroll=devs <= 8)
         def _(p):
             pltpu.make_async_remote_copy(
-                src_ref=e_recv.at[step, h, dev],
-                dst_ref=e_recv.at[step, h, dev],
+                src_ref=e_recv.at[step, h, dev // 2],
+                dst_ref=e_recv.at[step, h, dev // 2],
                 send_sem=send_sem.at[1, step, h],
                 recv_sem=recv_sem.at[1, step, h],
-                device_id=(area, lax.rem(dev + p, devs)),
+                device_id=(area, dev ^ (devs - 2 * p)),
                 device_id_type=MESH,
             ).start()
 
     def settle(step, h):
-        wait(e_recv.at[step, h], devs - 1, recv_sem.at[1, step, h])
-        opened = jnp.sum(e_recv[step, h], axis=0)
+        wait(e_recv.at[step, h], devs // 2 - 1, recv_sem.at[1, step, h])
+        own = lax.rem(dev, 2)
+        e_pair[step, h, own] = jnp.sum(e_recv[step, h], axis=0)
+        swap_sum = pltpu.make_async_remote_copy(
+            src_ref=e_pair.at[step, h, own],
+            dst_ref=e_pair.at[step, h, own],
+            send_sem=send_sem.at[3, step, h],
+            recv_sem=recv_sem.at[3, step, h],
+            device_id=(area, dev ^ 1),
+            device_id_type=MESH,
+        )
+        swap_sum.start()
+        swap_sum.wait()
+        opened = e_pair[step, h, 0] + e_pair[step, h, 1]
         result = jnp.dot(
             u[...], jnp.concatenate(high_low(opened), axis=1), preferred_element_type=F32
         )
@@ -517,9 +534,9 @@
 
     form_links()
     eliminate(near_inv)
-    for h in range(HALVES):
-        share(0, h)
+    share(0, 0)
     reduce_far()
+    share(0, 1)
     eliminate(far_inv)
     link_effect()
     for h in range(HALVES):
@@ -537,6 +554,7 @@
                 arr[h, m] = nxt[h, m] + moved[m]
             inject(step, h)
             push_all(h_send, h_recv, 0, step, h)
+        share(step, 0)
         for m in range(3):
             scatter(m)
         advance()
@@ -545,8 +563,7 @@
         def _():
             gather(nxt)
 
-        for h in range(HALVES):
-            share(step, h)
+        share(step, 1)
         for h in range(HALVES):
             settle(step, h)
         volt_copy(step).start()
@@ -569,7 +586,7 @@
         volt_copy(step).wait()
         for h in range(HALVES):
             wait(h_send.at[step, h], total - 1, send_sem.at[0, step, h])
-            wait(e_recv.at[step, h], devs - 1, send_sem.at[1, step, h])
+            wait(e_recv.at[step, h], devs // 2 - 1, send_sem.at[1, step, h])
             wait(v_send.at[step, h], total - 1, send_sem.at[2, step, h])
 
     for copy in outputs:
@@ -645,7 +662,8 @@
             pltpu.VMEM(volt_shape, F32),
             pltpu.VMEM(sent, F32),
             pltpu.VMEM(sent, F32),
-            pltpu.VMEM((STEPS, HALVES, devs, 3 * links // 2, cases), F32),
+            pltpu.VMEM((STEPS, HALVES, devs // 2, 3 * links // 2, cases), F32),
+            pltpu.VMEM((STEPS, HALVES, 2, 3 * links // 2, cases), F32),
             pltpu.VMEM(sent, F32),
             pltpu.VMEM(sent, F32),
             pltpu.VMEM((devs, 3, 3, buses), F32),
@@ -671,8 +689,8 @@
             pltpu.VMEM((HALVES, 3, buses // 2, cases), F32),
             *[pltpu.VMEM((3 * links // 2, 3 * links // 2), F32)] * 5,
             pltpu.VMEM((3, links, 2 * cases), F32),
-            pltpu.SemaphoreType.DMA((3, STEPS, HALVES)),
-            pltpu.SemaphoreType.DMA((3, STEPS, HALVES)),
+            pltpu.SemaphoreType.DMA((4, STEPS, HALVES)),
+            pltpu.SemaphoreType.DMA((4, STEPS, HALVES)),
             pltpu.SemaphoreType.DMA((2,)),
             pltpu.SemaphoreType.DMA((3,)),
             pltpu.SemaphoreType.DMA((STEPS + 6,)),

time: 108 us -> 105 us (0.972)
  Pallas kernels: 108 us -> 104 us
    pallas_call x1, Pallas kernels: 105 us -> 102 us  [on_device(): pl.pallas_call(functools.partial(kernel, areas, devs), out_shape=(jax.Sha...]
where the time goes in v3:
time: 105 us
  Pallas kernels  104 us (99%)
    pallas_call x1, Pallas kernels, on_device(): pl.pallas_call(functools.partial(kernel, areas, devs), out_shape=(jax.Sha...  102 us
    pallas_call x1, Pallas kernels, on_device(): pl.pallas_call(hand_over, out_shape=tuple((jax.ShapeDtypeStruct(a.shape,...  2.42 us

profile of v3, /device:TPU:0, one launch (start us, length us, event | category | flops | bytes accessed | tf_op | source)
XLA Modules:
  0.0 105.0 jit_solution(2283658623064857931)
XLA Ops:
  0.6 101.9 %transient.1 = (f32[4,3,64,128]{3,2,1,0:T(8,128)}, f32[3,512,128]{2,1,0:T(8,128)}, f32[3,512,128]{2,1,0:T(8,128)}) custom-call(f32[3,512,128]{2,1,0:T(8,128)} %fwd_in.1, f32[3,512,128]{2,1,0:T(8,128)} %bwd_in.1, f32[3,512]{1,0:T(4,128)} %refl_ref.1, s32[1,64]{1,0:T(1,128)} %count_ref.1, f32[3,64]{1,0:T(4,128)} %admit_ref.1, f32[3,3]{1,0:T(4,128)} %trans_ref.1, ...), custom_call_target="tpu_custom_call" | custom-call | tf_op jit(solution)/shard_map/transient/pallas_call | solution.py:649
  102.6 2.4 %hand_over.1 = (f32[4,3,64,128]{3,2,1,0:T(8,128)}, f32[3,512,128]{2,1,0:T(8,128)}, f32[3,512,128]{2,1,0:T(8,128)}) custom-call(f32[4,3,64,128]{3,2,1,0:T(8,128)} %get-tuple-element.9.volt_in, f32[3,512,128]{2,1,0:T(8,128)} %get-tuple-element.10.fwd_in, f32[3,512,128]{2,1,0:T(8,128)} %get-tuple-element.11.bwd_in), custom_call_target="tpu_custom_call" | custom-call | tf_op jit(solution)/shard_map/hand_over/pallas_call | solution.py:716

commit v4 on v3

--- a/solution.py
+++ b/solution.py
@@ -301,11 +301,12 @@
         zpack[ij] = jnp.where(lower(wide[:near]), wide[:near], wide[near:])
     inputs[2].wait()
 
-    @pl.loop(0, STEPS)
-    def _(step):
+    def pack_source(step):
         for i in range(3):
             for h, half in enumerate(pack(src[step, i])):
                 spack[step, h, i] = half
+
+    pack_source(0)
 
     def wave_tables():
         first_row, last_row = to_row(first_col), to_row(last_col)
@@ -485,7 +486,7 @@
                 device_id_type=MESH,
             ).start()
 
-    def settle(step, h):
+    def settle(step, h, meanwhile=None):
         wait(e_recv.at[step, h], devs // 2 - 1, recv_sem.at[1, step, h])
         own = lax.rem(dev, 2)
         e_pair[step, h, own] = jnp.sum(e_recv[step, h], axis=0)
@@ -498,6 +499,8 @@
             device_id_type=MESH,
         )
         swap_sum.start()
+        if meanwhile is not None:
+            meanwhile()
         swap_sum.wait()
         opened = e_pair[step, h, 0] + e_pair[step, h, 1]
         result = jnp.dot(
@@ -554,18 +557,14 @@
                 arr[h, m] = nxt[h, m] + moved[m]
             inject(step, h)
             push_all(h_send, h_recv, 0, step, h)
+        pack_source(step)
         share(step, 0)
         for m in range(3):
             scatter(m)
         advance()
-
-        @pl.when(step < STEPS - 1)
-        def _():
-            gather(nxt)
-
         share(step, 1)
-        for h in range(HALVES):
-            settle(step, h)
+        settle(step, 0, lambda: pl.when(step < STEPS - 1)(lambda: gather(nxt)))
+        settle(step, 1)
         volt_copy(step).start()
 
     for h in range(HALVES):

time: 105 us -> 105 us (level)
  no operation moved by 1% of the time
where the time goes in v4:
time: 105 us
  Pallas kernels  104 us (99%)
    pallas_call x1, Pallas kernels, on_device(): pl.pallas_call(functools.partial(kernel, areas, devs), out_shape=(jax.Sha...  102 us
    pallas_call x1, Pallas kernels, on_device(): pl.pallas_call(hand_over, out_shape=tuple((jax.ShapeDtypeStruct(a.shape,...  2.42 us

profile of v4, /device:TPU:0, one launch (start us, length us, event | category | flops | bytes accessed | tf_op | source)
XLA Modules:
  0.0 104.9 jit_solution(8724954988556606309)
XLA Ops:
  0.6 101.9 %transient.1 = (f32[4,3,64,128]{3,2,1,0:T(8,128)}, f32[3,512,128]{2,1,0:T(8,128)}, f32[3,512,128]{2,1,0:T(8,128)}) custom-call(f32[3,512,128]{2,1,0:T(8,128)} %fwd_in.1, f32[3,512,128]{2,1,0:T(8,128)} %bwd_in.1, f32[3,512]{1,0:T(4,128)} %refl_ref.1, s32[1,64]{1,0:T(1,128)} %count_ref.1, f32[3,64]{1,0:T(4,128)} %admit_ref.1, f32[3,3]{1,0:T(4,128)} %trans_ref.1, ...), custom_call_target="tpu_custom_call" | custom-call | tf_op jit(solution)/shard_map/transient/pallas_call | solution.py:648
  102.5 2.4 %hand_over.1 = (f32[4,3,64,128]{3,2,1,0:T(8,128)}, f32[3,512,128]{2,1,0:T(8,128)}, f32[3,512,128]{2,1,0:T(8,128)}) custom-call(f32[4,3,64,128]{3,2,1,0:T(8,128)} %get-tuple-element.9.volt_in, f32[3,512,128]{2,1,0:T(8,128)} %get-tuple-element.10.fwd_in, f32[3,512,128]{2,1,0:T(8,128)} %get-tuple-element.11.bwd_in), custom_call_target="tpu_custom_call" | custom-call | tf_op jit(solution)/shard_map/hand_over/pallas_call | solution.py:715
